TPU v7x, 32 devices: a whole 2x2x4 slice. The times are simulated.
32 devices in a mesh: row: 4 (over y, x), col: 2 (over core), depth: 4 (over z).
Axes of the slice: x: 2, y: 2, z: 4, core: 2. Of those that a mesh axis runs over, the one named last changes fastest.
Arguments:
- inputs: bfloat16 [1024, 12288], P(('col', 'depth'), 'row'), may hold values from -6 to 6
- weight: bfloat16 [12288, 49152], P('row', ('col', 'depth')), may hold values from -0.0546875 to 0.0546875
- out_grad: bfloat16 [1024, 49152], P('row', ('col', 'depth')), may hold values from -6 to 6
Outputs:
- activated: bfloat16 [1024, 49152], P('row', ('col', 'depth'))
- input_grad: bfloat16 [1024, 12288], P(('col', 'depth'), 'row')
- weight_grad: bfloat16 [12288, 49152], P('row', ('col', 'depth'))
All inputs are finite; a program needn't handle non-finite values.
Results may differ from a plain program's by a relative error of at most 0.0049.
Values may be sent and summed in bfloat16 or wider, within the bound.
A program may use at most 256 MiB of HBM per device.

v0:
```python
import math

import jax
import jax.numpy as jnp
from jax import lax
from jax.sharding import PartitionSpec as P

gelu_coef = 0.044715


def gelu_pair(pre, cotangent):
    scale = math.sqrt(2.0 / math.pi)
    inner = scale * (pre + gelu_coef * pre * pre * pre)
    tanh_val = jnp.tanh(inner)
    activated = (0.5 * pre * (1.0 + tanh_val)).astype(jnp.bfloat16)
    slope = 0.5 * (1.0 + tanh_val) + 0.5 * pre * (1.0 - tanh_val * tanh_val) * scale * (
        1.0 + 3.0 * gelu_coef * pre * pre
    )
    pre_grad = (cotangent.astype(jnp.float32) * slope).astype(jnp.bfloat16)
    return (activated, pre_grad)


def body(inputs, weight, out_grad):
    gathered = lax.all_gather(inputs, ("col", "depth"), axis=0, tiled=True)
    partial_pre = jnp.dot(gathered, weight, preferred_element_type=jnp.float32)
    pre = lax.psum_scatter(partial_pre, "row", scatter_dimension=0, tiled=True)
    activated, pre_grad = gelu_pair(pre, out_grad)
    grad_all = lax.all_gather(pre_grad, "row", axis=0, tiled=True)
    weight_grad = lax.dot_general(
        gathered, grad_all, (((0,), (0,)), ((), ())), preferred_element_type=jnp.float32
    ).astype(jnp.bfloat16)
    input_grad = lax.psum_scatter(
        lax.dot_general(
            grad_all, weight, (((1,), (1,)), ((), ())), preferred_element_type=jnp.float32
        ),
        ("col", "depth"),
        scatter_dimension=0,
        tiled=True,
    )
    return (activated, input_grad.astype(jnp.bfloat16), weight_grad)


def solution(mesh):
    return jax.shard_map(
        body,
        mesh=mesh,
        in_specs=(
            P(("col", "depth"), "row"),
            P("row", ("col", "depth")),
            P("row", ("col", "depth")),
        ),
        out_specs=(
            P("row", ("col", "depth")),
            P(("col", "depth"), "row"),
            P("row", ("col", "depth")),
        ),
        check_vma=False,
    )
```

profile of v0, /device:TPU:0, one launch (start us, length us, event | category | flops | bytes accessed | tf_op | source)
XLA Modules:
  0.0 777.7 jit_solution(4740505444279216994)
XLA Ops:
  7.2 0.0 all-gather.3.cloned.1.call-start
  7.2 0.7 all-gather.3.cloned.1.call-update
  7.9 0.0 reduce-scatter.3.cloned.1.call-start
  7.9 69.1 %all-gather.3.cloned.1.call-done = bf16[1024,3072]{1,0:T(8,128)(2,1)} async-done(((bf16[128,3072]{1,0:T(8,128)(2,1)}), bf16[1024,3072]{1,0:T(8,128)(2,1)}) %all-gather.3.cloned.1.call-update) | async-done | bytes 6291472 | tf_op jit(solution)/shard_map/all_gather | solution.py:24
  77.1 46.6 %fusion.7 = f32[1024,6144]{1,0:T(8,128)} fusion(bf16[1024,3072]{1,0:T(8,128)(2,1)} %all-gather.3.cloned.1.call-done, bf16[3072,6144]{1,0:T(8,128)(2,1)} %param.4), kind=kOutput, calls=%fused_computation.11 | convolution fusion | flops 38654705664 | bytes 69206016 | tf_op jit(solution)/shard_map/dot_general | solution.py:25
  123.7 0.0 copy-start
  123.7 0.0 reduce-scatter.3.cloned.1.call-update
  123.7 0.0 all-gather.5.cloned.1.call-start
  123.7 220.6 %reduce-scatter.3.cloned.1.call-done = f32[256,6144]{1,0:T(8,128)} async-done(((f32[1024,6144]{1,0:T(8,128)}), f32[256,6144]{1,0:T(8,128)}) %reduce-scatter.3.cloned.1.call-update) | async-done | bytes 6291472 | tf_op jit(solution)/shard_map/reduce_scatter | solution.py:26
  344.4 0.0 copy-done
  344.4 8.0 %fusion.6 = (bf16[256,6144]{1,0:T(8,128)(2,1)}, bf16[256,6144]{1,0:T(8,128)(2,1)}) fusion(f32[256,6144]{1,0:T(8,128)} %reduce-scatter.3.cloned.1.call-done, bf16[256,6144]{1,0:T(8,128)(2,1)S(1)} %copy-done), kind=kLoop, calls=%fused_computation.9 | loop fusion | flops 34603008 | bytes 15728640 | tf_op jit(solution)/shard_map/convert_element_type | solution.py:19
  352.4 0.0 all-gather.5.cloned.1.call-update
  352.4 0.2 reduce-scatter.5.cloned.1.call-start
  352.7 122.4 %all-gather.5.cloned.1.call-done = bf16[1024,6144]{1,0:T(8,128)(2,1)} async-done(((bf16[256,6144]{1,0:T(8,128)(2,1)}), bf16[1024,6144]{1,0:T(8,128)(2,1)}) %all-gather.5.cloned.1.call-update) | async-done | bytes 12582928 | tf_op jit(solution)/shard_map/all_gather | solution.py:28
  475.1 47.9 %fusion.8 = f32[1024,3072]{1,0:T(8,128)} fusion(bf16[1024,6144]{1,0:T(8,128)(2,1)} %all-gather.5.cloned.1.call-done, bf16[3072,6144]{1,0:T(8,128)(2,1)} %param.4), kind=kOutput, calls=%fused_computation.12 | convolution fusion | flops 38654705664 | bytes 62914560 | tf_op jit(solution)/shard_map/dot_general | solution.py:33
  523.0 0.0 reduce-scatter.5.cloned.1.call-update
  523.1 49.9 %convert_bitcast_fusion = bf16[3072,6144]{0,1:T(8,128)(2,1)} fusion(bf16[1024,6144]{1,0:T(8,128)(2,1)} %all-gather.5.cloned.1.call-done, bf16[1024,3072]{1,0:T(8,128)(2,1)} %all-gather.3.cloned.1.call-done), kind=kOutput, calls=%fused_computation | convolution fusion | flops 38673580032 | bytes 56623104 | tf_op jit(solution)/shard_map/dot_general | solution.py:29
  572.9 48.6 %copy.6 = bf16[3072,6144]{1,0:T(8,128)(2,1)} copy(bf16[3072,6144]{0,1:T(8,128)(2,1)} %convert_bitcast_fusion) | data formatting | bytes 75497472
  621.5 147.3 %reduce-scatter.5.cloned.1.call-done = f32[128,3072]{1,0:T(8,128)} async-done(((f32[1024,3072]{1,0:T(8,128)}), f32[128,3072]{1,0:T(8,128)}) %reduce-scatter.5.cloned.1.call-update) | async-done | bytes 1572880 | tf_op jit(solution)/shard_map/reduce_scatter | solution.py:32
  768.8 2.4 convert_element_type.21
Async XLA Ops:
  7.2 69.9 %all-gather.3.cloned.1.call-start = ((), (), s32[]{:S(2)}) async-start(), calls=%async_computation.2 | async-start | bytes 7077888 | tf_op jit(solution)/shard_map/all_gather | solution.py:24
  7.9 336.5 %reduce-scatter.3.cloned.1.call-start = ((), (), s32[]{:S(2)}) async-start(), calls=%async_computation.3 | async-start | bytes 31457280 | tf_op jit(solution)/shard_map/reduce_scatter | solution.py:26
  123.7 220.7 %copy-start = (bf16[256,6144]{1,0:T(8,128)(2,1)S(1)}, bf16[256,6144]{1,0:T(8,128)(2,1)}, u32[]{:S(2)}) copy-start(bf16[256,6144]{1,0:T(8,128)(2,1)} %param.5) | copy-start | bytes 9437188
  123.7 351.4 %all-gather.5.cloned.1.call-start = ((), (), s32[]{:S(2)}) async-start(), calls=%async_computation.4 | async-start | bytes 15728640 | tf_op jit(solution)/shard_map/all_gather | solution.py:28
  352.4 416.4 %reduce-scatter.5.cloned.1.call-start = ((), (), s32[]{:S(2)}) async-start(), calls=%async_computation.5 | async-start | bytes 14155776 | tf_op jit(solution)/shard_map/reduce_scatter | solution.py:32
Sparse Core Ops, SparseCore 0:
  9.6 67.4 all-gather.2
  123.8 220.5 reduce-scatter.2
  352.5 122.4 all-gather.4
  523.2 245.5 reduce-scatter.4
where the time goes:
time: 779 us; the launch traced here: 778 us
  waiting for transfers between devices  560 us (72%)
  matrix products  144 us (18%)
  local copies, waits for them, and re-layouts  48.6 us (6%)
  between operations  13.8 us (2%)
  other arithmetic  10.4 us (1%)
    reduce_scatter x1, waiting for transfers between devices, body(): pre = lax.psum_scatter(partial_pre, 'row', scatter_dimension=0, tiled=True)  221 us
    reduce_scatter x1, waiting for transfers between devices, body(): lax.psum_scatter(lax.dot_general(grad_all, weight, (((1,), (1,)), ((), ()...  147 us
    all_gather x1, waiting for transfers between devices, body(): grad_all = lax.all_gather(pre_grad, 'row', axis=0, tiled=True)  122 us
    all_gather x1, waiting for transfers between devices, body(): gathered = lax.all_gather(inputs, ('col', 'depth'), axis=0, tiled=True)  69.1 us
    dot_general x1, matrix products, body(): lax.dot_general(gathered, grad_all, (((0,), (0,)), ((), ())), preferred_e...  49.9 us
    unnamed x3, local copies, waits for them, and re-layouts  48.6 us
    dot_general x1, matrix products, body(): lax.dot_general(grad_all, weight, (((1,), (1,)), ((), ())), preferred_ele...  47.9 us
    dot_general x1, matrix products, body(): partial_pre = jnp.dot(gathered, weight, preferred_element_type=jnp.float32)  46.6 us
  transfers between devices with their start and end apart: 4, of which 4 were waited for; matrix products, arithmetic and copies ran while one was open for 13% of the time, Pallas kernels for 0%

commit v1 on v0

v1 whole, which is shorter than its diff:
```python
import functools
import math

import jax
import jax.numpy as jnp
from jax import lax
from jax.experimental import pallas as pl
from jax.experimental.pallas import tpu as pltpu
from jax.sharding import PartitionSpec as P

gelu_coef = 0.044715
HALVES = 2


def gelu_pair(pre, cotangent):
    scale = math.sqrt(2.0 / math.pi)
    inner = scale * (pre + gelu_coef * pre * pre * pre)
    tanh_val = jnp.tanh(inner)
    activated = (0.5 * pre * (1.0 + tanh_val)).astype(jnp.bfloat16)
    slope = 0.5 * (1.0 + tanh_val) + 0.5 * pre * (1.0 - tanh_val * tanh_val) * scale * (
        1.0 + 3.0 * gelu_coef * pre * pre
    )
    pre_grad = (cotangent.astype(jnp.float32) * slope).astype(jnp.bfloat16)
    return (activated, pre_grad)


def weight_grad_kernel(*refs):
    out_ref = refs[-1]
    xs = refs[:HALVES]
    gs = refs[HALVES : 2 * HALVES]
    total = jnp.dot(xs[0][...], gs[0][...], preferred_element_type=jnp.float32)
    for x, g in zip(xs[1:], gs[1:]):
        total += jnp.dot(x[...], g[...], preferred_element_type=jnp.float32)
    out_ref[...] = total.astype(out_ref.dtype)


def weight_grad_columns(xts, gs, chunk, full_shape, dest):
    rows = full_shape[0]
    width = gs[0].shape[1]
    depth = gs[0].shape[0]
    bm = 512
    bn = width // 2 if width % 256 == 0 else width
    per = width // bn
    in_specs = [pl.BlockSpec((bm, depth), lambda j, i: (i, 0)) for _ in xts]
    in_specs += [pl.BlockSpec((depth, bn), lambda j, i: (0, j)) for _ in gs]
    operands = list(xts) + list(gs)
    aliases = {}
    if dest is not None:
        aliases = {len(operands): 0}
        operands.append(dest)
        in_specs.append(pl.BlockSpec(memory_space=pl.ANY))
    flops = 2 * rows * width * depth * len(xts)
    return pl.pallas_call(
        weight_grad_kernel,
        out_shape=jax.ShapeDtypeStruct(full_shape, jnp.bfloat16),
        grid=(per, rows // bm),
        in_specs=in_specs,
        out_specs=pl.BlockSpec((bm, bn), lambda j, i: (i, chunk * per + j)),
        input_output_aliases=aliases,
        compiler_params=pltpu.CompilerParams(vmem_limit_bytes=40 * 1024 * 1024),
        cost_estimate=pl.CostEstimate(
            flops=flops, bytes_accessed=2 * rows * width + 4 * rows * depth, transcendentals=0
        ),
    )(*operands)


def swap(x, flip):
    return lax.ppermute(x, "row", [(i, i ^ flip) for i in range(4)])


def pick(x, axis, index):
    return lax.dynamic_index_in_dim(x, index, axis, keepdims=False)


def placed(mine, other, bit, axis):
    first = jnp.where(bit == 0, mine, other)
    second = jnp.where(bit == 0, other, mine)
    return jnp.stack([first, second], axis=axis)


def reduce_rows(part, by, bx, x_first):
    if x_first:
        got = swap(pick(part, 1, 1 - bx), 1)
        kept, bit, flip = pick(part, 1, bx), by, 2
    else:
        got = swap(pick(part, 0, 1 - by), 2)
        kept, bit, flip = pick(part, 0, by), bx, 1
    send = pick(kept, 0, 1 - bit).astype(jnp.float32) + pick(got, 0, 1 - bit).astype(jnp.float32)
    last = swap(send.astype(jnp.bfloat16), flip)
    own = pick(kept, 0, bit).astype(jnp.float32) + pick(got, 0, bit).astype(jnp.float32)
    return own + last.astype(jnp.float32)


def gather_rows(g, by, bx, x_first):
    over_y = swap(g, 2)
    over_x = swap(g, 1)
    diagonal = swap(over_y, 1) if x_first else swap(over_x, 2)
    same_x = placed(g, over_y, by, 0)
    other_x = placed(over_x, diagonal, by, 0)
    full = placed(same_x, other_x, bx, 1)
    return full.reshape((-1, g.shape[-1]))


def scatter_sum(part, cols, depths):
    width = part.shape[1]
    part = part.reshape((cols, depths, -1, width))
    me_c, me_d = lax.axis_index("col"), lax.axis_index("depth")
    if cols != 2 or depths > 4:
        flat = part.reshape((-1, width)).astype(jnp.float32)
        return lax.psum_scatter(flat, ("col", "depth"), scatter_dimension=0, tiled=True)
    got = lax.ppermute(pick(part, 0, 1 - me_c).astype(jnp.bfloat16), "col", [(0, 1), (1, 0)])
    kept = pick(part, 0, me_c) + got.astype(jnp.float32)
    ring = [(i, (i + 1) % depths) for i in range(depths)]
    acc = pick(kept, 0, (me_d + depths - 1) % depths)
    for step in range(depths - 1):
        got = lax.ppermute(acc.astype(jnp.bfloat16), "depth", ring)
        acc = got.astype(jnp.float32) + pick(kept, 0, (me_d + 2 * depths - 2 - step) % depths)
    return acc


def body(inputs, weight, out_grad, *, cols, depths):
    tok, d_in = inputs.shape
    own_rows, hidden = out_grad.shape
    m = tok // HALVES
    per_row = own_rows // tok
    chunks = 4 if hidden % 2048 == 0 else 2
    width = hidden // chunks
    row = lax.axis_index("row")
    by, bx = row // 2, row % 2

    xs = [
        lax.all_gather(inputs[h * m : (h + 1) * m], ("col", "depth"), axis=0, tiled=True)
        for h in range(HALVES)
    ]
    xts = [x.T for x in xs]
    og = out_grad.reshape((per_row, HALVES, m, hidden))
    activated = [[None] * chunks for _ in range(HALVES)]
    grads = [[None] * chunks for _ in range(HALVES)]
    sums = []
    wg = None
    for h in range(HALVES):
        total = None
        for c in range(chunks):
            cut = slice(c * width, (c + 1) * width)
            part = jnp.dot(xs[h], weight[:, cut], preferred_element_type=jnp.float32)
            part = part.astype(jnp.bfloat16).reshape((2, 2, -1, width))
            pre = reduce_rows(part, by, bx, c % 2 == 0)
            cot = og[:, h, :, cut].reshape(pre.shape)
            activated[h][c], g = gelu_pair(pre, cot)
            grads[h][c] = gather_rows(g, by, bx, c % 2 == 0)
            term = lax.dot_general(
                grads[h][c],
                weight[:, cut],
                (((1,), (1,)), ((), ())),
                preferred_element_type=jnp.float32,
            )
            total = term if total is None else total + term
            if h == HALVES - 1:
                wg = weight_grad_columns(
                    xts, [grads[k][c] for k in range(HALVES)], c, (d_in, hidden), wg
                )
        sums.append(scatter_sum(total, cols, depths).astype(jnp.bfloat16))
    act = jnp.stack(
        [
            jnp.concatenate(activated[h], axis=1).reshape((per_row, m, hidden))
            for h in range(HALVES)
        ],
        axis=1,
    ).reshape((own_rows, hidden))
    return (act, jnp.concatenate(sums, axis=0), wg)


def solution(mesh):
    return jax.shard_map(
        functools.partial(body, cols=mesh.shape["col"], depths=mesh.shape["depth"]),
        mesh=mesh,
        in_specs=(
            P(("col", "depth"), "row"),
            P("row", ("col", "depth")),
            P("row", ("col", "depth")),
        ),
        out_specs=(
            P("row", ("col", "depth")),
            P(("col", "depth"), "row"),
            P("row", ("col", "depth")),
        ),
        check_vma=False,
    )
```

time: 779 us -> 568 us (0.73)
  waiting for transfers between devices: 560 us -> 217 us
  Pallas kernels: 0 us -> 52.7 us
  starting transfers between devices: 0.34 us -> 44.3 us
  other arithmetic: 10.4 us -> 37.5 us
  matrix products: 144 us -> 163 us
  local copies, waits for them, and re-layouts: 48.6 us -> 30.1 us
    reduce_scatter x2 -> x0, waiting for transfers between devices: 368 us -> none  [the longest x1 221 us: body(): pre = lax.psum_scatter(partial_pre, 'row', scatter_dimension=0, tiled=True)]
    ppermute x0 -> x48, waiting for transfers between devices: none -> 178 us  [the longest x40 128 us: swap(): return lax.ppermute(x, 'row', [(i, i ^ flip) for i in range(4)])]
    all_gather x2, waiting for transfers between devices: 192 us -> 37.7 us  [body(): lax.all_gather(inputs[h * m:(h + 1) * m], ('col', 'depth'), axis=0, tiled...]
    pallas_call x0 -> x4, Pallas kernels: none -> 52.7 us  [weight_grad_columns(): pl.pallas_call(weight_grad_kernel, out_shape=jax.ShapeDtypeStruct(full_sh...]
    unnamed x3 -> x76, local copies, waits for them, and re-layouts: 48.6 us -> 1.65 us
    ppermute x0 -> x48, starting transfers between devices: none -> 44.2 us  [the longest x40 41.5 us: swap(): return lax.ppermute(x, 'row', [(i, i ^ flip) for i in range(4)])]
    dot_general x3 -> x16, matrix products: 144 us -> 163 us  [the longest x8 96 us: body(): lax.dot_general(grads[h][c], weight[:, cut], (((1,), (1,)), ((), ())), pr...]
    another operation x0 -> x25, other arithmetic: none -> 12.1 us  [the longest x24 10.2 us: placed(): return jnp.stack([first, second], axis=axis)]
  transfers between devices with their start and end apart: 4 -> 50, of which waited for: 4 -> 21; matrix products, arithmetic and copies ran while one was open for 13% -> 40% of each run, Pallas kernels for 0% -> 9%
where the time goes in v1:
time: 568 us; the launch traced here: 560 us
  waiting for transfers between devices  217 us (38%)
  matrix products  163 us (29%)
  Pallas kernels  52.7 us (9%)
  starting transfers between devices  44.3 us (8%)
  other arithmetic  37.5 us (7%)
  local copies, waits for them, and re-layouts  30.1 us (5%)
  between operations  15.4 us (3%)
    ppermute x40, waiting for transfers between devices, swap(): return lax.ppermute(x, 'row', [(i, i ^ flip) for i in range(4)])  128 us
    dot_general x8, matrix products, body(): lax.dot_general(grads[h][c], weight[:, cut], (((1,), (1,)), ((), ())), pr...  96 us
    dot_general x8, matrix products, body(): part = jnp.dot(xs[h], weight[:, cut], preferred_element_type=jnp.float32)  67.4 us
    pallas_call x4, Pallas kernels, weight_grad_columns(): pl.pallas_call(weight_grad_kernel, out_shape=jax.ShapeDtypeStruct(full_sh...  52.7 us
    ppermute x6, waiting for transfers between devices, scatter_sum(): got = lax.ppermute(acc.astype(jnp.bfloat16), 'depth', ring)  50.4 us
    ppermute x40, starting transfers between devices, swap(): return lax.ppermute(x, 'row', [(i, i ^ flip) for i in range(4)])  41.5 us
    all_gather x2, waiting for transfers between devices, body(): lax.all_gather(inputs[h * m:(h + 1) * m], ('col', 'depth'), axis=0, tiled...  37.7 us
    convert_element_type x8, other arithmetic, gelu_pair(): pre_grad = (cotangent.astype(jnp.float32) * slope).astype(jnp.bfloat16)  12.6 us
  transfers between devices with their start and end apart: 50, of which 21 were waited for; matrix products, arithmetic and copies ran while one was open for 40% of the time, Pallas kernels for 9%

profile of v1, /device:TPU:0, one launch (start us, length us, event | category | flops | bytes accessed | tf_op | source)
XLA Modules:
  0.0 559.9 jit_solution(10444302177955164095)
XLA Ops:
  13.5 37.7 %all-gather.5.cloned.1.call-done = bf16[512,3072]{1,0:T(8,128)(2,1)} async-done(((bf16[64,3072]{1,0:T(8,128)(2,1)}), bf16[512,3072]{1,0:T(8,128)(2,1)}) %all-gather.5.cloned.1.call-update) | async-done | bytes 3145744 | tf_op jit(solution)/shard_map/all_gather | solution.py:132
  51.2 9.5 %fusion.57 = bf16[512,1536]{1,0:T(8,128)(2,1)S(1)} fusion(bf16[512,3072]{1,0:T(8,128)(2,1)} %all-gather.5.cloned.1.call-done, bf16[3072,6144]{1,0:T(8,128)(2,1)} %param.4), kind=kOutput, calls=%fused_computation.46 | convolution fusion | flops 4832624640 | bytes 14155776 | tf_op jit(solution)/shard_map/dot_general | solution.py:145
  74.0 7.8 %fusion.45 = bf16[512,1536]{1,0:T(8,128)(2,1)S(1)} fusion(bf16[512,3072]{1,0:T(8,128)(2,1)S(1)} %copy-done.7, bf16[3072,6144]{1,0:T(8,128)(2,1)} %param.4), kind=kOutput, calls=%fused_computation.42 | convolution fusion | flops 4832624640 | bytes 14155776 | tf_op jit(solution)/shard_map/dot_general | solution.py:145
  93.9 9.5 %fusion.54 = bf16[512,1536]{1,0:T(8,128)(2,1)S(1)} fusion(bf16[512,3072]{1,0:T(8,128)(2,1)} %all-gather.3.cloned.1.call-done, bf16[3072,6144]{1,0:T(8,128)(2,1)} %param.4), kind=kOutput, calls=%fused_computation.45 | convolution fusion | flops 4832624640 | bytes 14155776 | tf_op jit(solution)/shard_map/dot_general | solution.py:145
  105.9 8.2 %fusion.48 = bf16[512,1536]{1,0:T(8,128)(2,1)S(1)} fusion(bf16[512,3072]{1,0:T(8,128)(2,1)S(1)} %copy-done.8, bf16[3072,6144]{1,0:T(8,128)(2,1)} %param.4), kind=kOutput, calls=%fused_computation.43 | convolution fusion | flops 4832624640 | bytes 14155776 | tf_op jit(solution)/shard_map/dot_general | solution.py:145
  114.2 8.3 %fusion.42 = bf16[512,1536]{1,0:T(8,128)(2,1)S(1)} fusion(bf16[512,3072]{1,0:T(8,128)(2,1)S(1)} %copy-done.8, bf16[3072,6144]{1,0:T(8,128)(2,1)} %param.4), kind=kOutput, calls=%fused_computation.41 | convolution fusion | flops 4832624640 | bytes 14155776 | tf_op jit(solution)/shard_map/dot_general | solution.py:145
  122.5 8.3 %fusion.36 = bf16[512,1536]{1,0:T(8,128)(2,1)S(1)} fusion(bf16[512,3072]{1,0:T(8,128)(2,1)S(1)} %copy-done.8, bf16[3072,6144]{1,0:T(8,128)(2,1)} %param.4), kind=kOutput, calls=%fused_computation.39 | convolution fusion | flops 4832624640 | bytes 14155776 | tf_op jit(solution)/shard_map/dot_general | solution.py:145
  153.7 11.8 %collective-permute-done.2 = bf16[2,128,1536]{2,1,0:T(8,128)(2,1)S(1)} collective-permute-done((bf16[2,128,1536]{2,1,0:T(8,128)(2,1)}, bf16[2,128,1536]{2,1,0:T(8,128)(2,1)S(1)}, u32[]{:S(2)}, u32[]{:S(2)}) %collective-permute-start.2) | collective-permute-done | bytes 786464 | tf_op jit(solution)/shard_map/ppermute | solution.py:68
  167.8 11.8 %collective-permute-done = bf16[2,128,1536]{2,1,0:T(8,128)(2,1)S(1)} collective-permute-done((bf16[2,128,1536]{2,1,0:T(8,128)(2,1)}, bf16[2,128,1536]{2,1,0:T(8,128)(2,1)S(1)}, u32[]{:S(2)}, u32[]{:S(2)}) %collective-permute-start) | collective-permute-done | bytes 786464 | tf_op jit(solution)/shard_map/ppermute | solution.py:68
  180.2 22.4 %collective-permute-done.3 = bf16[128,1536]{1,0:T(8,128)(2,1)S(1)} collective-permute-done((bf16[128,1536]{1,0:T(8,128)(2,1)S(1)}, bf16[128,1536]{1,0:T(8,128)(2,1)S(1)}, u32[]{:S(2)}, u32[]{:S(2)}) %collective-permute-start.3) | collective-permute-done | bytes 393248 | tf_op jit(solution)/shard_map/ppermute | solution.py:68
  203.9 8.0 %collective-permute-done.5 = bf16[128,1536]{1,0:T(8,128)(2,1)S(1)} collective-permute-done((bf16[128,1536]{1,0:T(8,128)(2,1)S(1)}, bf16[128,1536]{1,0:T(8,128)(2,1)S(1)}, u32[]{:S(2)}, u32[]{:S(2)}) %collective-permute-start.5) | collective-permute-done | bytes 393248 | tf_op jit(solution)/shard_map/ppermute | solution.py:68
  222.2 8.0 %collective-permute-done.7 = bf16[128,1536]{1,0:T(8,128)(2,1)S(1)} collective-permute-done((bf16[128,1536]{1,0:T(8,128)(2,1)S(1)}, bf16[128,1536]{1,0:T(8,128)(2,1)S(1)}, u32[]{:S(2)}, u32[]{:S(2)}) %collective-permute-start.7) | collective-permute-done | bytes 393248 | tf_op jit(solution)/shard_map/ppermute | solution.py:68
  253.4 13.1 %collective-permute-done.38 = bf16[128,1536]{1,0:T(8,128)(2,1)} collective-permute-done((bf16[128,1536]{1,0:T(8,128)(2,1)}, bf16[128,1536]{1,0:T(8,128)(2,1)}, u32[]{:S(2)}, u32[]{:S(2)}) %collective-permute-start.38) | collective-permute-done | bytes 393248 | tf_op jit(solution)/shard_map/ppermute | solution.py:68
  269.1 9.1 %collective-permute-done.35 = bf16[128,1536]{1,0:T(8,128)(2,1)S(1)} collective-permute-done((bf16[128,1536]{1,0:T(8,128)(2,1)S(1)}, bf16[128,1536]{1,0:T(8,128)(2,1)S(1)}, u32[]{:S(2)}, u32[]{:S(2)}) %collective-permute-start.35) | collective-permute-done | bytes 393248 | tf_op jit(solution)/shard_map/ppermute | solution.py:68
  278.4 11.1 %collective-permute-done.32 = bf16[128,1536]{1,0:T(8,128)(2,1)} collective-permute-done((bf16[128,1536]{1,0:T(8,128)(2,1)}, bf16[128,1536]{1,0:T(8,128)(2,1)}, u32[]{:S(2)}, u32[]{:S(2)}) %collective-permute-start.32) | collective-permute-done | bytes 393248 | tf_op jit(solution)/shard_map/ppermute | solution.py:68
  318.9 10.9 %fusion.18 = f32[512,3072]{1,0:T(8,128)} fusion(bf16[512,1536]{1,0:T(8,128)(2,1)S(1)} %bitcast.308, bf16[3072,6144]{1,0:T(8,128)(2,1)} %param.4), kind=kOutput, calls=%fused_computation.20 | convolution fusion | flops 4831838208 | bytes 17301504 | tf_op jit(solution)/shard_map/dot_general | solution.py:151
  333.0 10.7 %fusion.10 = f32[512,3072]{1,0:T(8,128)} fusion(bf16[512,1536]{1,0:T(8,128)(2,1)S(1)} %bitcast.310, bf16[3072,6144]{1,0:T(8,128)(2,1)} %param.4), kind=kOutput, calls=%fused_computation.12 | convolution fusion | flops 4831838208 | bytes 17301504 | tf_op jit(solution)/shard_map/dot_general | solution.py:151
  345.0 10.7 %fusion.2 = f32[512,3072]{1,0:T(8,128)} fusion(bf16[512,1536]{1,0:T(8,128)(2,1)S(1)} %bitcast.312, bf16[3072,6144]{1,0:T(8,128)(2,1)} %param.4), kind=kOutput, calls=%fused_computation.4 | convolution fusion | flops 4831838208 | bytes 17301504 | tf_op jit(solution)/shard_map/dot_general | solution.py:151
  366.4 15.3 %add_add_fusion.1 = f32[512,3072]{1,0:T(8,128)} fusion(f32[512,3072]{1,0:T(8,128)} %fusion.2, f32[512,3072]{1,0:T(8,128)} %fusion.10, f32[512,3072]{1,0:T(8,128)} %fusion.18, bf16[512,1536]{1,0:T(8,128)(2,1)S(1)} %bitcast.304, bf16[3072,6144]{1,0:T(8,128)(2,1)} %param.4), kind=kOutput, calls=%fused_computation.1 | convolution fusion | flops 4836556800 | bytes 36175872 | tf_op jit(solution)/shard_map/dot_general | solution.py:151
  381.7 10.7 %fusion.16 = f32[512,3072]{1,0:T(8,128)} fusion(bf16[512,1536]{1,0:T(8,128)(2,1)S(1)} %bitcast.314, bf16[3072,6144]{1,0:T(8,128)(2,1)} %param.4), kind=kOutput, calls=%fused_computation.18 | convolution fusion | flops 4831838208 | bytes 17301504 | tf_op jit(solution)/shard_map/dot_general | solution.py:151
  397.3 11.5 %fusion.8 = f32[512,3072]{1,0:T(8,128)} fusion(bf16[512,1536]{1,0:T(8,128)(2,1)S(1)} %bitcast.316, bf16[3072,6144]{1,0:T(8,128)(2,1)} %param.4), kind=kOutput, calls=%fused_computation.10 | convolution fusion | flops 4831838208 | bytes 17301504 | tf_op jit(solution)/shard_map/dot_general | solution.py:151
  410.3 11.3 %fusion = f32[512,3072]{1,0:T(8,128)} fusion(bf16[512,1536]{1,0:T(8,128)(2,1)S(1)} %bitcast.318, bf16[3072,6144]{1,0:T(8,128)(2,1)} %param.4), kind=kOutput, calls=%fused_computation.2 | convolution fusion | flops 4831838208 | bytes 17301504 | tf_op jit(solution)/shard_map/dot_general | solution.py:151
  423.1 14.9 %add_add_fusion = f32[512,3072]{1,0:T(8,128)} fusion(f32[512,3072]{1,0:T(8,128)} %fusion, f32[512,3072]{1,0:T(8,128)} %fusion.8, f32[512,3072]{1,0:T(8,128)} %fusion.16, bf16[512,1536]{1,0:T(8,128)(2,1)S(1)} %bitcast.306, bf16[3072,6144]{1,0:T(8,128)(2,1)} %param.4), kind=kOutput, calls=%fused_computation | convolution fusion | flops 4836556800 | bytes 36175872 | tf_op jit(solution)/shard_map/dot_general | solution.py:151
  441.9 13.2 %shard_map.58.refs_4_ = bf16[3072,6144]{1,0:T(8,128)(2,1)} custom-call(bf16[3072,512]{1,0:T(8,128)(2,1)S(1)} %bitcast.300, bf16[3072,512]{1,0:T(8,128)(2,1)S(1)} %bitcast.296, bf16[512,1536]{1,0:T(8,128)(2,1)S(1)} %bitcast.305, bf16[512,1536]{1,0:T(8,128)(2,1)S(1)} %bitcast.307), custom_call_target="tpu_custom_call" | custom-call | flops 9663676416 | bytes 15728640 | tf_op jit(solution)/shard_map/pallas_call | solution.py:53
  455.1 13.2 %shard_map.59.refs_4_ = bf16[3072,6144]{1,0:T(8,128)(2,1)} custom-call(bf16[3072,512]{1,0:T(8,128)(2,1)S(1)} %bitcast.301, bf16[3072,512]{1,0:T(8,128)(2,1)S(1)} %bitcast.297, bf16[512,1536]{1,0:T(8,128)(2,1)S(1)} %bitcast.309, bf16[512,1536]{1,0:T(8,128)(2,1)S(1)} %bitcast.315, bf16[3072,6144]{1,0:T(8,128)(2,1)} %shard_map.58.refs_4_), custom_call_target="tpu_custom_call", output_to_operand_aliasing={{}: (4, {})} | custom-call | flops 9663676416 | bytes 15728640 | tf_op jit(solution)/shard_map/pallas_call | solution.py:53
  468.2 13.2 %shard_map.60.refs_4_ = bf16[3072,6144]{1,0:T(8,128)(2,1)} custom-call(bf16[3072,512]{1,0:T(8,128)(2,1)S(1)} %bitcast.302, bf16[3072,512]{1,0:T(8,128)(2,1)S(1)} %bitcast.298, bf16[512,1536]{1,0:T(8,128)(2,1)S(1)} %bitcast.311, bf16[512,1536]{1,0:T(8,128)(2,1)S(1)} %bitcast.317, bf16[3072,6144]{1,0:T(8,128)(2,1)} %shard_map.59.refs_4_), custom_call_target="tpu_custom_call", output_to_operand_aliasing={{}: (4, {})} | custom-call | flops 9663676416 | bytes 15728640 | tf_op jit(solution)/shard_map/pallas_call | solution.py:53
  481.5 13.2 %shard_map.61 = bf16[3072,6144]{1,0:T(8,128)(2,1)} custom-call(bf16[3072,512]{1,0:T(8,128)(2,1)S(1)} %bitcast.303, bf16[3072,512]{1,0:T(8,128)(2,1)S(1)} %bitcast.299, bf16[512,1536]{1,0:T(8,128)(2,1)S(1)} %bitcast.313, bf16[512,1536]{1,0:T(8,128)(2,1)S(1)} %bitcast.319, bf16[3072,6144]{1,0:T(8,128)(2,1)} %shard_map.60.refs_4_), custom_call_target="tpu_custom_call", output_to_operand_aliasing={{}: (4, {})} | custom-call | flops 9663676416 | bytes 15728640 | tf_op jit(solution)/shard_map/pallas_call | solution.py:53
  500.5 9.9 %collective-permute-done.29 = bf16[64,3072]{1,0:T(8,128)(2,1)S(1)} collective-permute-done((bf16[64,3072]{1,0:T(8,128)(2,1)S(1)}, bf16[64,3072]{1,0:T(8,128)(2,1)S(1)}, u32[]{:S(2)}, u32[]{:S(2)}) %collective-permute-start.29) | collective-permute-done | bytes 393248 | tf_op jit(solution)/shard_map/ppermute | solution.py:116
  510.6 8.3 %collective-permute-done.45 = bf16[64,3072]{1,0:T(8,128)(2,1)S(1)} collective-permute-done((bf16[64,3072]{1,0:T(8,128)(2,1)S(1)}, bf16[64,3072]{1,0:T(8,128)(2,1)S(1)}, u32[]{:S(2)}, u32[]{:S(2)}) %collective-permute-start.45) | collective-permute-done | bytes 393248 | tf_op jit(solution)/shard_map/ppermute | solution.py:116
  519.0 8.3 %collective-permute-done.30 = bf16[64,3072]{1,0:T(8,128)(2,1)S(1)} collective-permute-done((bf16[64,3072]{1,0:T(8,128)(2,1)S(1)}, bf16[64,3072]{1,0:T(8,128)(2,1)S(1)}, u32[]{:S(2)}, u32[]{:S(2)}) %collective-permute-start.30) | collective-permute-done | bytes 393248 | tf_op jit(solution)/shard_map/ppermute | solution.py:116
  527.4 8.3 %collective-permute-done.46 = bf16[64,3072]{1,0:T(8,128)(2,1)S(1)} collective-permute-done((bf16[64,3072]{1,0:T(8,128)(2,1)S(1)}, bf16[64,3072]{1,0:T(8,128)(2,1)S(1)}, u32[]{:S(2)}, u32[]{:S(2)}) %collective-permute-start.46) | collective-permute-done | bytes 393248 | tf_op jit(solution)/shard_map/ppermute | solution.py:116
  535.9 8.3 %collective-permute-done.31 = bf16[64,3072]{1,0:T(8,128)(2,1)S(1)} collective-permute-done((bf16[64,3072]{1,0:T(8,128)(2,1)S(1)}, bf16[64,3072]{1,0:T(8,128)(2,1)S(1)}, u32[]{:S(2)}, u32[]{:S(2)}) %collective-permute-start.31) | collective-permute-done | bytes 393248 | tf_op jit(solution)/shard_map/ppermute | solution.py:116
  (244 shorter events, 168.2 us)
Async XLA Ops:
  7.2 44.0 %all-gather.5.cloned.1.call-start = ((), (), s32[]{:S(2)}) async-start(), calls=%async_computation.1 | async-start | bytes 3538944 | tf_op jit(solution)/shard_map/all_gather | solution.py:132
  9.3 84.6 %all-gather.3.cloned.1.call-start = ((), (), s32[]{:S(2)}) async-start(), calls=%async_computation | async-start | bytes 3538944 | tf_op jit(solution)/shard_map/all_gather | solution.py:132
  62.1 79.8 %collective-permute-start.14 = (bf16[2,128,1536]{2,1,0:T(8,128)(2,1)}, bf16[2,128,1536]{2,1,0:T(8,128)(2,1)}, u32[]{:S(2)}, u32[]{:S(2)}) collective-permute-start(bf16[2,128,1536]{2,1,0:T(8,128)(2,1)} %dynamic-slice_bitcast_fusion), channel_id=1, source_target_pairs={{0,16},{8,24},{16,0},{24,8},{1,17},{9,25},{17,1},{25,9},{2,18},{10... | collective-permute-start | bytes 2359304 | tf_op jit(solution)/shard_map/ppermute | solution.py:68
  72.5 74.0 %collective-permute-start.12 = (bf16[2,128,1536]{2,1,0:T(8,128)(2,1)}, bf16[2,128,1536]{2,1,0:T(8,128)(2,1)}, u32[]{:S(2)}, u32[]{:S(2)}) collective-permute-start(bf16[2,128,1536]{2,1,0:T(8,128)(2,1)} %dynamic-slice_bitcast_fusion.1), channel_id=1, source_target_pairs={{0,8},{8,0},{16,24},{24,16},{1,9},{9,1},{17,25},{25,17},{2,10},{10... | collective-permute-start | bytes 2359304 | tf_op jit(solution)/shard_map/ppermute | solution.py:68
  82.9 61.8 %collective-permute-start.10 = (bf16[2,128,1536]{2,1,0:T(8,128)(2,1)}, bf16[2,128,1536]{2,1,0:T(8,128)(2,1)}, u32[]{:S(2)}, u32[]{:S(2)}) collective-permute-start(bf16[2,128,1536]{2,1,0:T(8,128)(2,1)} %dynamic-slice_bitcast_fusion.2), channel_id=1, source_target_pairs={{0,16},{8,24},{16,0},{24,8},{1,17},{9,25},{17,1},{25,9},{2,18},{10... | collective-permute-start | bytes 2359304 | tf_op jit(solution)/shard_map/ppermute | solution.py:68
  93.3 55.5 %collective-permute-start.8 = (bf16[2,128,1536]{2,1,0:T(8,128)(2,1)}, bf16[2,128,1536]{2,1,0:T(8,128)(2,1)}, u32[]{:S(2)}, u32[]{:S(2)}) collective-permute-start(bf16[2,128,1536]{2,1,0:T(8,128)(2,1)} %dynamic-slice_bitcast_fusion.3), channel_id=1, source_target_pairs={{0,8},{8,0},{16,24},{24,16},{1,9},{9,1},{17,25},{25,17},{2,10},{10... | collective-permute-start | bytes 2359304 | tf_op jit(solution)/shard_map/ppermute | solution.py:68
  104.5 46.5 %collective-permute-start.6 = (bf16[2,128,1536]{2,1,0:T(8,128)(2,1)}, bf16[2,128,1536]{2,1,0:T(8,128)(2,1)}, u32[]{:S(2)}, u32[]{:S(2)}) collective-permute-start(bf16[2,128,1536]{2,1,0:T(8,128)(2,1)} %dynamic-slice_bitcast_fusion.4), channel_id=1, source_target_pairs={{0,16},{8,24},{16,0},{24,8},{1,17},{9,25},{17,1},{25,9},{2,18},{10... | collective-permute-start | bytes 2359304 | tf_op jit(solution)/shard_map/ppermute | solution.py:68
  142.0 24.5 %collective-permute-start.4 = (bf16[2,128,1536]{2,1,0:T(8,128)(2,1)}, bf16[2,128,1536]{2,1,0:T(8,128)(2,1)S(1)}, u32[]{:S(2)}, u32[]{:S(2)}) collective-permute-start(bf16[2,128,1536]{2,1,0:T(8,128)(2,1)} %dynamic-slice_bitcast_fusion.5), channel_id=1, source_target_pairs={{0,8},{8,0},{16,24},{24,16},{1,9},{9,1},{17,25},{25,17},{2,10},{10... | collective-permute-start | bytes 2359304 | tf_op jit(solution)/shard_map/ppermute | solution.py:68
  144.8 20.8 %collective-permute-start.2 = (bf16[2,128,1536]{2,1,0:T(8,128)(2,1)}, bf16[2,128,1536]{2,1,0:T(8,128)(2,1)S(1)}, u32[]{:S(2)}, u32[]{:S(2)}) collective-permute-start(bf16[2,128,1536]{2,1,0:T(8,128)(2,1)} %dynamic-slice_bitcast_fusion.6), channel_id=1, source_target_pairs={{0,16},{8,24},{16,0},{24,8},{1,17},{9,25},{17,1},{25,9},{2,18},{10... | collective-permute-start | bytes 2359304 | tf_op jit(solution)/shard_map/ppermute | solution.py:68
  146.5 33.1 %collective-permute-start = (bf16[2,128,1536]{2,1,0:T(8,128)(2,1)}, bf16[2,128,1536]{2,1,0:T(8,128)(2,1)S(1)}, u32[]{:S(2)}, u32[]{:S(2)}) collective-permute-start(bf16[2,128,1536]{2,1,0:T(8,128)(2,1)} %dynamic-slice_bitcast_fusion.7), channel_id=1, source_target_pairs={{0,8},{8,0},{16,24},{24,16},{1,9},{9,1},{17,25},{25,17},{2,10},{10... | collective-permute-start | bytes 2359304 | tf_op jit(solution)/shard_map/ppermute | solution.py:68
  148.8 84.7 %collective-permute-start.15 = (bf16[128,1536]{1,0:T(8,128)(2,1)S(1)}, bf16[128,1536]{1,0:T(8,128)(2,1)S(1)}, u32[]{:S(2)}, u32[]{:S(2)}) collective-permute-start(bf16[128,1536]{1,0:T(8,128)(2,1)S(1)} %fusion.118), channel_id=1, source_target_pairs={{0,8},{8,0},{16,24},{24,16},{1,9},{9,1},{17,25},{25,17},{2,10},{10... | collective-permute-start | bytes 1179656 | tf_op jit(solution)/shard_map/ppermute | solution.py:68
  151.0 91.4 %collective-permute-start.13 = (bf16[128,1536]{1,0:T(8,128)(2,1)S(1)}, bf16[128,1536]{1,0:T(8,128)(2,1)S(1)}, u32[]{:S(2)}, u32[]{:S(2)}) collective-permute-start(bf16[128,1536]{1,0:T(8,128)(2,1)S(1)} %fusion.120), channel_id=1, source_target_pairs={{0,16},{8,24},{16,0},{24,8},{1,17},{9,25},{17,1},{25,9},{2,18},{10... | collective-permute-start | bytes 1179656 | tf_op jit(solution)/shard_map/ppermute | solution.py:68
  165.5 73.6 %collective-permute-start.11 = (bf16[128,1536]{1,0:T(8,128)(2,1)S(1)}, bf16[128,1536]{1,0:T(8,128)(2,1)S(1)}, u32[]{:S(2)}, u32[]{:S(2)}) collective-permute-start(bf16[128,1536]{1,0:T(8,128)(2,1)S(1)} %fusion.122), channel_id=1, source_target_pairs={{0,8},{8,0},{16,24},{24,16},{1,9},{9,1},{17,25},{25,17},{2,10},{10... | collective-permute-start | bytes 1179656 | tf_op jit(solution)/shard_map/ppermute | solution.py:68
  166.5 36.2 %collective-permute-start.3 = (bf16[128,1536]{1,0:T(8,128)(2,1)S(1)}, bf16[128,1536]{1,0:T(8,128)(2,1)S(1)}, u32[]{:S(2)}, u32[]{:S(2)}) collective-permute-start(bf16[128,1536]{1,0:T(8,128)(2,1)S(1)} %fusion.130), channel_id=1, source_target_pairs={{0,8},{8,0},{16,24},{24,16},{1,9},{9,1},{17,25},{25,17},{2,10},{10... | collective-permute-start | bytes 1179656 | tf_op jit(solution)/shard_map/ppermute | solution.py:68
  179.6 56.4 %collective-permute-start.9 = (bf16[128,1536]{1,0:T(8,128)(2,1)S(1)}, bf16[128,1536]{1,0:T(8,128)(2,1)S(1)}, u32[]{:S(2)}, u32[]{:S(2)}) collective-permute-start(bf16[128,1536]{1,0:T(8,128)(2,1)S(1)} %fusion.124), channel_id=1, source_target_pairs={{0,16},{8,24},{16,0},{24,8},{1,17},{9,25},{17,1},{25,9},{2,18},{10... | collective-permute-start | bytes 1179656 | tf_op jit(solution)/shard_map/ppermute | solution.py:68
  230.2 125.6 %collective-permute-start.17 = (bf16[128,1536]{1,0:T(8,128)(2,1)S(1)}, bf16[128,1536]{1,0:T(8,128)(2,1)S(1)}, u32[]{:S(2)}, u32[]{:S(2)}) collective-permute-start(bf16[128,1536]{1,0:T(8,128)(2,1)S(1)} %get-tuple-element.11), channel_id=1, source_target_pairs={{0,8},{8,0},{16,24},{24,16},{1,9},{9,1},{17,25},{25,17},{2,10},{10... | collective-permute-start | bytes 1179656 | tf_op jit(solution)/shard_map/ppermute | solution.py:68
  236.0 122.7 %collective-permute-start.42 = (bf16[128,1536]{1,0:T(8,128)(2,1)S(1)}, bf16[128,1536]{1,0:T(8,128)(2,1)}, u32[]{:S(2)}, u32[]{:S(2)}) collective-permute-start(bf16[128,1536]{1,0:T(8,128)(2,1)S(1)} %get-tuple-element.25), channel_id=1, source_target_pairs={{0,8},{8,0},{16,24},{24,16},{1,9},{9,1},{17,25},{25,17},{2,10},{10... | collective-permute-start | bytes 1179656 | tf_op jit(solution)/shard_map/ppermute | solution.py:68
  242.4 87.4 %collective-permute-start.26 = (bf16[128,1536]{1,0:T(8,128)(2,1)S(1)}, bf16[128,1536]{1,0:T(8,128)(2,1)S(1)}, u32[]{:S(2)}, u32[]{:S(2)}) collective-permute-start(bf16[128,1536]{1,0:T(8,128)(2,1)S(1)} %get-tuple-element.17), channel_id=1, source_target_pairs={{0,8},{8,0},{16,24},{24,16},{1,9},{9,1},{17,25},{25,17},{2,10},{10... | collective-permute-start | bytes 1179656 | tf_op jit(solution)/shard_map/ppermute | solution.py:68
  248.6 43.5 %collective-permute-start.25 = (bf16[128,1536]{1,0:T(8,128)(2,1)S(1)}, bf16[128,1536]{1,0:T(8,128)(2,1)S(1)}, u32[]{:S(2)}, u32[]{:S(2)}) collective-permute-start(bf16[128,1536]{1,0:T(8,128)(2,1)S(1)} %get-tuple-element.17), channel_id=1, source_target_pairs={{0,16},{8,24},{16,0},{24,8},{1,17},{9,25},{17,1},{25,9},{2,18},{10... | collective-permute-start | bytes 1179656 | tf_op jit(solution)/shard_map/ppermute | solution.py:68
  300.8 29.3 %collective-permute-start.23 = (bf16[128,1536]{1,0:T(8,128)(2,1)S(1)}, bf16[128,1536]{1,0:T(8,128)(2,1)S(1)}, u32[]{:S(2)}, u32[]{:S(2)}) collective-permute-start(bf16[128,1536]{1,0:T(8,128)(2,1)S(1)} %get-tuple-element.15), channel_id=1, source_target_pairs={{0,8},{8,0},{16,24},{24,16},{1,9},{9,1},{17,25},{25,17},{2,10},{10... | collective-permute-start | bytes 1179656 | tf_op jit(solution)/shard_map/ppermute | solution.py:68
  329.8 65.9 %collective-permute-start.39 = (bf16[128,1536]{1,0:T(8,128)(2,1)}, bf16[128,1536]{1,0:T(8,128)(2,1)}, u32[]{:S(2)}, u32[]{:S(2)}) collective-permute-start(bf16[128,1536]{1,0:T(8,128)(2,1)} %get-tuple-element.23), channel_id=1, source_target_pairs={{0,8},{8,0},{16,24},{24,16},{1,9},{9,1},{17,25},{25,17},{2,10},{10... | collective-permute-start | bytes 1179656 | tf_op jit(solution)/shard_map/ppermute | solution.py:68
  330.0 26.8 %collective-permute-start.36 = (bf16[128,1536]{1,0:T(8,128)(2,1)S(1)}, bf16[128,1536]{1,0:T(8,128)(2,1)S(1)}, u32[]{:S(2)}, u32[]{:S(2)}) collective-permute-start(bf16[128,1536]{1,0:T(8,128)(2,1)S(1)} %get-tuple-element.21), channel_id=1, source_target_pairs={{0,8},{8,0},{16,24},{24,16},{1,9},{9,1},{17,25},{25,17},{2,10},{10... | collective-permute-start | bytes 1179656 | tf_op jit(solution)/shard_map/ppermute | solution.py:68
  355.7 65.9 %collective-permute-start.33 = (bf16[128,1536]{1,0:T(8,128)(2,1)}, bf16[128,1536]{1,0:T(8,128)(2,1)}, u32[]{:S(2)}, u32[]{:S(2)}) collective-permute-start(bf16[128,1536]{1,0:T(8,128)(2,1)} %get-tuple-element.19), channel_id=1, source_target_pairs={{0,8},{8,0},{16,24},{24,16},{1,9},{9,1},{17,25},{25,17},{2,10},{10... | collective-permute-start | bytes 1179656 | tf_op jit(solution)/shard_map/ppermute | solution.py:68
  356.8 38.9 %collective-permute-start.40 = (bf16[128,1536]{1,0:T(8,128)(2,1)}, bf16[128,1536]{1,0:T(8,128)(2,1)}, u32[]{:S(2)}, u32[]{:S(2)}) collective-permute-start(bf16[128,1536]{1,0:T(8,128)(2,1)} %collective-permute-done.38), channel_id=1, source_target_pairs={{0,8},{8,0},{16,24},{24,16},{1,9},{9,1},{17,25},{25,17},{2,10},{10... | collective-permute-start | bytes 1179656 | tf_op jit(solution)/shard_map/ppermute | solution.py:68
  358.7 62.9 %collective-permute-start.34 = (bf16[128,1536]{1,0:T(8,128)(2,1)}, bf16[128,1536]{1,0:T(8,128)(2,1)}, u32[]{:S(2)}, u32[]{:S(2)}) collective-permute-start(bf16[128,1536]{1,0:T(8,128)(2,1)} %collective-permute-done.32), channel_id=1, source_target_pairs={{0,8},{8,0},{16,24},{24,16},{1,9},{9,1},{17,25},{25,17},{2,10},{10... | collective-permute-start | bytes 1179656 | tf_op jit(solution)/shard_map/ppermute | solution.py:68
  365.5 43.2 %collective-permute-start.43 = (bf16[128,1536]{1,0:T(8,128)(2,1)}, bf16[128,1536]{1,0:T(8,128)(2,1)}, u32[]{:S(2)}, u32[]{:S(2)}) collective-permute-start(bf16[128,1536]{1,0:T(8,128)(2,1)} %collective-permute-done.42), channel_id=1, source_target_pairs={{0,16},{8,24},{16,0},{24,8},{1,17},{9,25},{17,1},{25,9},{2,18},{10... | collective-permute-start | bytes 1179656 | tf_op jit(solution)/shard_map/ppermute | solution.py:68
  395.8 98.9 %collective-permute-start.28 = (bf16[4,64,3072]{2,1,0:T(8,128)(2,1)}, bf16[4,64,3072]{2,1,0:T(8,128)(2,1)}, u32[]{:S(2)}, u32[]{:S(2)}) collective-permute-start(bf16[4,64,3072]{2,1,0:T(8,128)(2,1)} %fusion.60), channel_id=1, source_target_pairs={{0,4},{4,0},{1,5},{5,1},{2,6},{6,2},{3,7},{7,3},{8,12},{12,8},{9,1... | collective-permute-start | bytes 4718600 | tf_op jit(solution)/shard_map/ppermute | solution.py:111
  441.4 55.8 %collective-permute-start.44 = (bf16[4,64,3072]{2,1,0:T(8,128)(2,1)}, bf16[4,64,3072]{2,1,0:T(8,128)(2,1)}, u32[]{:S(2)}, u32[]{:S(2)}) collective-permute-start(bf16[4,64,3072]{2,1,0:T(8,128)(2,1)} %fusion.61), channel_id=1, source_target_pairs={{0,4},{4,0},{1,5},{5,1},{2,6},{6,2},{3,7},{7,3},{8,12},{12,8},{9,1... | collective-permute-start | bytes 4718600 | tf_op jit(solution)/shard_map/ppermute | solution.py:111
  499.2 19.7 %collective-permute-start.45 = (bf16[64,3072]{1,0:T(8,128)(2,1)S(1)}, bf16[64,3072]{1,0:T(8,128)(2,1)S(1)}, u32[]{:S(2)}, u32[]{:S(2)}) collective-permute-start(bf16[64,3072]{1,0:T(8,128)(2,1)S(1)} %fusion.141), channel_id=1, source_target_pairs={{0,1},{1,2},{2,3},{3,0},{4,5},{5,6},{6,7},{7,4},{8,9},{9,10},{10,1... | collective-permute-start | bytes 1179656 | tf_op jit(solution)/shard_map/ppermute | solution.py:116
  510.5 16.8 %collective-permute-start.30 = (bf16[64,3072]{1,0:T(8,128)(2,1)S(1)}, bf16[64,3072]{1,0:T(8,128)(2,1)S(1)}, u32[]{:S(2)}, u32[]{:S(2)}) collective-permute-start(bf16[64,3072]{1,0:T(8,128)(2,1)S(1)} %fusion.139), channel_id=1, source_target_pairs={{0,1},{1,2},{2,3},{3,0},{4,5},{5,6},{6,7},{7,4},{8,9},{9,10},{10,1... | collective-permute-start | bytes 1179656 | tf_op jit(solution)/shard_map/ppermute | solution.py:116
  519.0 16.8 %collective-permute-start.46 = (bf16[64,3072]{1,0:T(8,128)(2,1)S(1)}, bf16[64,3072]{1,0:T(8,128)(2,1)S(1)}, u32[]{:S(2)}, u32[]{:S(2)}) collective-permute-start(bf16[64,3072]{1,0:T(8,128)(2,1)S(1)} %fusion.136), channel_id=1, source_target_pairs={{0,1},{1,2},{2,3},{3,0},{4,5},{5,6},{6,7},{7,4},{8,9},{9,10},{10,1... | collective-permute-start | bytes 1179656 | tf_op jit(solution)/shard_map/ppermute | solution.py:116
  527.4 16.8 %collective-permute-start.31 = (bf16[64,3072]{1,0:T(8,128)(2,1)S(1)}, bf16[64,3072]{1,0:T(8,128)(2,1)S(1)}, u32[]{:S(2)}, u32[]{:S(2)}) collective-permute-start(bf16[64,3072]{1,0:T(8,128)(2,1)S(1)} %fusion.138), channel_id=1, source_target_pairs={{0,1},{1,2},{2,3},{3,0},{4,5},{5,6},{6,7},{7,4},{8,9},{9,10},{10,1... | collective-permute-start | bytes 1179656 | tf_op jit(solution)/shard_map/ppermute | solution.py:116
  (56 other events, 823.0 us)
Sparse Core Ops, SparseCore 0:
  10.2 40.9 all-gather.4
  52.8 37.1 all-gather.2
